TPU v7x, 32 devices: a whole 2x2x4 slice. The times are simulated.
32 devices in a mesh: sec: 2 (over y), tube: 4 (over z), blk: 2 (over x), sub: 2 (over core).
Axes of the slice: x: 2, y: 2, z: 4, core: 2. Of those that a mesh axis runs over, the one named last changes fastest.
Arguments:
- latent: float32 [2048, 256], P(('sec', 'tube'), 'blk'), parts along dimension 0, may hold values from 0.2 to 5
- weight_maps: bfloat16 [8, 2048, 256], P('sub', ('sec', 'tube'), 'blk'), parts along dimension 1, may hold values from 0.039794922 to 0.19921875
- row_taps: float32 [8, 31], P('sub'), may hold values from 0.05 to 1
- col_taps: float32 [8, 31], P('sub'), may hold values from 0.05 to 1
- exposures: bfloat16 [2, 512, 128, 128], P('blk', ('sec', 'tube')), parts along dimension 1, may hold values from 0.19921875 to 5
- gains: bfloat16 [2, 512], P('blk', ('sec', 'tube')), parts along dimension 1, may hold values from 0.5 to 2
- owners: int32 [2, 512, 1], P('blk', ('sec', 'tube')), parts along dimension 1, may hold values from 0 to 3, as said below
- offsets: int32 [2, 512], P('blk', ('sec', 'tube')), parts along dimension 1, may hold values from 0 to 1, as said below
Outputs:
- updated: float32 [2048, 256], P(('sec', 'tube'), 'blk'), parts along dimension 0
There are 2 independent parts, one for each index of `sec`. A program takes and returns all parts, laid end to end along the dimension named above; an argument that names none is the same for every part. Nothing has to cross between parts.
Inputs may be any that keep to these rules, and one draw needn't show every extreme that they name: `owners`: among the 64 slots of one device no tube position is named more than 32 times; in each column of blocks some tube position is named exactly 32 times by every device of that column. `offsets`: some block places of the image receive no slot.
All inputs are finite; a program needn't handle non-finite values.
Results may differ from a plain program's by a relative error of at most 0.00035.
Values may be sent and summed in bfloat16 or wider, within the bound.
A program may use at most 64 MiB of HBM per device.

v0:
```python
import jax
import jax.numpy as jnp
from jax import lax
from jax.sharding import PartitionSpec as P


def extended(block, sides, width, periodic):
    for axis, dim in sides:
        count = lax.axis_size(axis)
        forward = [(i, i + 1) for i in range(count - 1)]
        if periodic:
            forward.append((count - 1, 0))
        backward = [(target, source) for source, target in forward]
        low = lax.ppermute(
            lax.slice_in_dim(block, block.shape[dim] - width, None, axis=dim), axis, forward
        )
        high = lax.ppermute(lax.slice_in_dim(block, 0, width, axis=dim), axis, backward)
        block = jnp.concatenate([low, block, high], axis=dim)
    return block


def sweep(source, tap_stack, length, dimension):
    running = tap_stack[0] * lax.slice_in_dim(source, 0, length, axis=dimension)
    for tap_index in range(1, tap_stack.shape[0]):
        running = running + tap_stack[tap_index] * lax.slice_in_dim(
            source, tap_index, tap_index + length, axis=dimension
        )
    return running


def separable(source, row_stack, col_stack, out_rows, out_cols):
    row_pass = sweep(source, row_stack, out_rows, source.ndim - 2)
    return sweep(row_pass, col_stack, out_cols, row_pass.ndim - 1)


def body(latent, weight_maps, row_taps, col_taps, exposures, gains, owners, offsets):
    tile_rows, block_size = latent.shape
    tap_count = row_taps.shape[1]
    margin = tap_count // 2
    row_blocks = tile_rows // block_size
    slot_count = exposures.shape[1]
    tube_count = lax.axis_size("tube")
    capacity = max(2, 2 * slot_count // tube_count)
    row_norm = row_taps / jnp.sum(row_taps, axis=1, keepdims=True)
    col_norm = col_taps / jnp.sum(col_taps, axis=1, keepdims=True)
    row_ahead = row_norm.T[:, :, None, None]
    col_ahead = col_norm.T[:, :, None, None]
    row_behind = row_norm[:, ::-1].T[:, :, None, None]
    col_behind = col_norm[:, ::-1].T[:, :, None, None]
    weight_stack = weight_maps.astype(jnp.float32)
    target = owners[0, :, 0]
    placement_plan = (offsets[0][:, None] == jnp.arange(row_blocks)[None, :]).astype(jnp.bfloat16)
    earlier = jnp.arange(slot_count)[None, :] < jnp.arange(slot_count)[:, None]
    matching = target[:, None] == target[None, :]
    order_rank = jnp.sum(matching & earlier, axis=1)
    picked_tube = (target[None, None, :] == jnp.arange(tube_count)[:, None, None]) & (
        order_rank[None, None, :] == jnp.arange(capacity)[None, :, None]
    )
    picked_tube = picked_tube.astype(jnp.bfloat16)
    send_blocks = jnp.einsum(
        "mew,wng->meng", picked_tube, exposures[0], preferred_element_type=jnp.float32
    ).astype(jnp.bfloat16)
    send_places = jnp.einsum(
        "jaf,fu->jau", picked_tube, placement_plan, preferred_element_type=jnp.float32
    ).astype(jnp.bfloat16)
    send_gains = jnp.einsum(
        "jaf,fu->jau",
        picked_tube,
        placement_plan * gains[0][:, None],
        preferred_element_type=jnp.float32,
    ).astype(jnp.bfloat16)
    got_blocks, received_positions, got_gains = (
        lax.all_to_all(send_blocks, "tube", split_axis=0, concat_axis=0, tiled=True),
        lax.all_to_all(send_places, "tube", split_axis=0, concat_axis=0, tiled=True),
        lax.all_to_all(send_gains, "tube", split_axis=0, concat_axis=0, tiled=True),
    )
    count_blocks = jnp.einsum(
        "tcr,tcxy->rxy", received_positions, got_blocks, preferred_element_type=jnp.float32
    )
    gain_blocks = jnp.sum(got_gains.astype(jnp.float32), axis=(0, 1))
    counts = count_blocks.reshape(tile_rows, block_size)
    coverage = jnp.broadcast_to(
        jnp.repeat(gain_blocks, block_size)[:, None], (tile_rows, block_size)
    )
    padded = extended(latent.astype(jnp.bfloat16), (("tube", 0),), margin, False).astype(
        latent.dtype
    )
    padded = extended(padded.astype(jnp.bfloat16), (("blk", 1),), margin, True).astype(padded.dtype)
    partial_value = jnp.sum(
        weight_stack * separable(padded[None], row_ahead, col_ahead, tile_rows, block_size), axis=0
    )
    smeared_image = lax.psum(partial_value.astype(jnp.bfloat16), "sub").astype(jnp.float32)
    quotient = counts / smeared_image
    stacked = jnp.stack([weight_stack * quotient[None], weight_stack * coverage[None]])
    weighted = extended(stacked, (("tube", 2),), margin, False)
    weighted = extended(weighted, (("blk", 3),), margin, True)
    backward = jnp.sum(separable(weighted, row_behind, col_behind, tile_rows, block_size), axis=1)
    numerator, denominator = lax.psum((backward[0], backward[1]), "sub")
    return latent * numerator / jnp.maximum(denominator, 0.25)


def solution(mesh):
    in_specs = (
        P(("sec", "tube"), "blk"),
        P("sub", ("sec", "tube"), "blk"),
        P("sub", None),
        P("sub", None),
        P("blk", ("sec", "tube"), None, None),
        P("blk", ("sec", "tube")),
        P("blk", ("sec", "tube"), None),
        P("blk", ("sec", "tube")),
    )
    out_specs = P(("sec", "tube"), "blk")
    return jax.shard_map(body, mesh=mesh, in_specs=in_specs, out_specs=out_specs, check_vma=False)
```

profile of v0, /device:TPU:0, one launch (start us, length us, event | category | flops | bytes accessed | tf_op | source)
XLA Modules:
  0.0 301.7 jit_solution(13113632499515899674)
XLA Ops:
  9.6 6.3 %all-to-all-start = ((bf16[4,32,2]{1,2,0:T(2,128)(2,1)}), bf16[4,32,2]{1,2,0:T(2,128)(2,1)S(1)}, u32[]{:S(2)}, u32[]{:S(2)}) async-start(bf16[4,32,2]{1,2,0:T(2,128)(2,1)} %convolution_convert_fusion.2), calls=%async_computation | async-start | bytes 4096 | tf_op jit(solution)/shard_map/all_to_all | solution.py:74
  17.3 4.1 %all-to-all-done = bf16[4,32,2]{1,2,0:T(2,128)(2,1)S(1)} async-done(((bf16[4,32,2]{1,2,0:T(2,128)(2,1)}), bf16[4,32,2]{1,2,0:T(2,128)(2,1)S(1)}, u32[]{:S(2)}, u32[]{:S(2)}) %all-to-all-start) | async-done | bytes 544 | tf_op jit(solution)/shard_map/all_to_all | solution.py:74
  21.4 3.2 %all-to-all-start.2 = ((bf16[4,32,2]{1,2,0:T(2,128)(2,1)}), bf16[4,32,2]{1,2,0:T(2,128)(2,1)S(1)}, u32[]{:S(2)}, u32[]{:S(2)}) async-start(bf16[4,32,2]{1,2,0:T(2,128)(2,1)} %convolution_convert_fusion.1), calls=%async_computation.2 | async-start | bytes 4096 | tf_op jit(solution)/shard_map/all_to_all | solution.py:75
  24.6 1.9 convolution_convert_fusion
  26.5 2.7 copy.88
  30.1 4.8 %all-to-all-start.1 = ((bf16[4,32,128,128]{3,1,2,0:T(8,128)(2,1)}), bf16[4,32,128,128]{3,1,2,0:T(8,128)(2,1)}, u32[]{:S(2)}, u32[]{:S(2)}) async-start(bf16[4,32,128,128]{3,1,2,0:T(8,128)(2,1)} %copy.88), calls=%async_computation.1 | async-start | bytes 8388608 | tf_op jit(solution)/shard_map/all_to_all | solution.py:73
  36.3 4.7 %collective-permute-start = (bf16[15,128]{1,0:T(8,128)(2,1)S(1)}, bf16[15,128]{1,0:T(8,128)(2,1)S(1)}, u32[]{:S(2)}, u32[]{:S(2)}) collective-permute-start(bf16[15,128]{1,0:T(8,128)(2,1)S(1)} %get-tuple-element.174), channel_id=1, source_target_pairs={{0,4},{4,8},{8,12},{1,5},{5,9},{9,13},{2,6},{6,10},{10,14},{3,7},{... | collective-permute-start | bytes 11528 | tf_op jit(solution)/shard_map/ppermute | solution.py:14
  46.6 33.9 %collective-permute-done.1 = bf16[15,128]{1,0:T(8,128)(2,1)S(1)} collective-permute-done((bf16[15,128]{1,0:T(8,128)(2,1)S(1)}, bf16[15,128]{1,0:T(8,128)(2,1)S(1)}, u32[]{:S(2)}, u32[]{:S(2)}) %collective-permute-start.1) | collective-permute-done | bytes 3872 | tf_op jit(solution)/shard_map/ppermute | solution.py:17
  80.6 20.3 %collective-permute-done = bf16[15,128]{1,0:T(8,128)(2,1)S(1)} collective-permute-done((bf16[15,128]{1,0:T(8,128)(2,1)S(1)}, bf16[15,128]{1,0:T(8,128)(2,1)S(1)}, u32[]{:S(2)}, u32[]{:S(2)}) %collective-permute-start) | collective-permute-done | bytes 3872 | tf_op jit(solution)/shard_map/ppermute | solution.py:14
  107.0 2.1 slice_bitcast_fusion.30
  145.0 1.8 copy.100
  157.4 10.0 %multiply_add_fusion = f32[4,256,158]{1,0,2:T(4,128)S(1)} fusion(f32[256,158]{0,1:T(8,128)S(1)} %copy-done.2, f32[4]{0:T(128)} %get-tuple-element.99, f32[256,158]{0,1:T(8,128)} %copy.120, f32[4]{0:T(128)} %get-tuple-element.100, f32[256,158]{0,1:T(8,128)} %copy.119, f32[4]{0:T(128)} %get-tuple-element.101, f32[256,158]{0,1:T(8,128)} %copy.118, ...), kind=kLoop, calls=%fused_computation.134 | loop fusion | flops 9869312 | bytes 5663216 | tf_op jit(solution)/shard_map/add | solution.py:25
  167.7 4.4 %fusion.62 = bf16[256,128]{0,1:T(8,128)(2,1)} fusion(bf16[4,256,128]{1,0,2:T(4,128)(2,1)S(1)} %copy.86, f32[4,256,158]{1,0,2:T(4,128)S(1)} %multiply_add_fusion, f32[4]{0:T(128)S(1)} %copy-done.15, f32[4]{0:T(128)S(1)} %copy-done.16, f32[4]{0:T(128)S(1)} %copy-done.17, f32[4]{0:T(128)S(1)} %copy-done.18, f32[4]{0:T(128)S(1)} %copy-done.19, ...), kind=kLoop, calls=%fused_computation.135 | loop fusion | flops 8355840 | bytes 16581104 | tf_op jit(solution)/shard_map/reduce_sum | solution.py:89
  172.3 2.9 convolution_bitcast_fusion
  175.3 37.7 %all-reduce.4.cloned.1.call-done = bf16[256,128]{0,1:T(8,128)(2,1)} async-done(((bf16[256,128]{0,1:T(8,128)(2,1)}), bf16[256,128]{0,1:T(8,128)(2,1)}) %all-reduce.4.cloned.1.call-update) | async-done | bytes 65552 | tf_op jit(solution)/shard_map/psum | solution.py:92
  215.8 4.8 %collective-permute-start.4 = (f32[2,4,15,128]{2,1,3,0:T(4,128)S(1)}, f32[2,4,15,128]{2,1,3,0:T(4,128)S(1)}, u32[]{:S(2)}, u32[]{:S(2)}) collective-permute-start(f32[2,4,15,128]{2,1,3,0:T(4,128)S(1)} %get-tuple-element.133), channel_id=1, source_target_pairs={{0,4},{4,8},{8,12},{1,5},{5,9},{9,13},{2,6},{6,10},{10,14},{3,7},{... | collective-permute-start | bytes 184328 | tf_op jit(solution)/shard_map/ppermute | solution.py:14
  221.0 9.6 %collective-permute-done.5 = f32[2,4,15,128]{2,1,3,0:T(4,128)S(1)} collective-permute-done((f32[2,4,15,128]{2,1,3,0:T(4,128)S(1)}, f32[2,4,15,128]{2,1,3,0:T(4,128)S(1)}, u32[]{:S(2)}, u32[]{:S(2)}) %collective-permute-start.5) | collective-permute-done | bytes 61472 | tf_op jit(solution)/shard_map/ppermute | solution.py:17
  232.0 1.8 collective-permute-start.7
  235.0 4.7 %collective-permute-done.7 = f32[2,4,286,15]{2,1,3,0:T(4,128)S(1)} collective-permute-done((f32[2,4,286,15]{2,1,3,0:T(4,128)S(1)}, f32[2,4,286,15]{2,1,3,0:T(4,128)S(1)}, u32[]{:S(2)}, u32[]{:S(2)}) %collective-permute-start.7) | collective-permute-done | bytes 137312 | tf_op jit(solution)/shard_map/ppermute | solution.py:17
  239.7 2.1 collective-permute-done.6
  241.8 2.6 pad_maximum_fusion
  244.3 20.9 %fusion.1 = f32[2,4,256,158]{2,1,3,0:T(4,128)S(1)} fusion(f32[2,4,286,158]{2,1,3,0:T(4,128)S(1)} %pad_maximum_fusion, f32[4]{0:T(128)S(1)} %get-tuple-element.37, f32[4]{0:T(128)S(1)} %get-tuple-element.38, f32[4]{0:T(128)S(1)} %get-tuple-element.39, f32[4]{0:T(128)S(1)} %get-tuple-element.40, f32[4]{0:T(128)S(1)} %get-tuple-element.41, ...), kind=kLoop, calls=%fused_computation.4 | loop fusion | flops 19738624 | bytes 41419248 | tf_op jit(solution)/shard_map/add | solution.py:25
  265.2 6.5 %fusion.32 = f32[2,256,128]{1,2,0:T(8,128)S(1)} fusion(f32[2,4,256,158]{2,1,3,0:T(4,128)S(1)} %fusion.1, f32[4]{0:T(128)S(1)} %get-tuple-element.6, f32[4]{0:T(128)S(1)} %get-tuple-element.7, f32[4]{0:T(128)S(1)} %get-tuple-element.8, f32[4]{0:T(128)S(1)} %get-tuple-element.9, f32[4]{0:T(128)S(1)} %get-tuple-element.10, f32[4]{0:T(128)S(1)} %get-tuple-element.11, ...), kind=kLoop, calls=%fused_computation.69 | loop fusion | flops 16187392 | bytes 32768496 | tf_op jit(solution)/shard_map/reduce_sum | solution.py:97
  272.6 20.5 %all-reduce.6.cloned.1.call-done = (f32[256,128]{0,1:T(8,128)}, f32[256,128]{0,1:T(8,128)}) async-done(((f32[256,128]{0,1:T(8,128)}, f32[256,128]{0,1:T(8,128)}), (f32[256,128]{0,1:T(8,128)}, f32[256,128]{0,1:T(8,128)})) %all-reduce.6.cloned.1.call-update) | async-done | bytes 262160 | tf_op jit(solution)/shard_map/psum | solution.py:98
  (152 shorter events, 73.2 us)
Async XLA Ops:
  6.5 18.1 %copy-start = (bf16[1,64,128,128]{3,2,1,0:T(8,128)(2,1)S(1)}, bf16[1,64,128,128]{3,2,1,0:T(8,128)(2,1)}, u32[]{:S(2)}) copy-start(bf16[1,64,128,128]{3,2,1,0:T(8,128)(2,1)} %param.12) | copy-start | bytes 6291460
  9.6 11.8 %all-to-all-start = ((bf16[4,32,2]{1,2,0:T(2,128)(2,1)}), bf16[4,32,2]{1,2,0:T(2,128)(2,1)S(1)}, u32[]{:S(2)}, u32[]{:S(2)}) async-start(bf16[4,32,2]{1,2,0:T(2,128)(2,1)} %convolution_convert_fusion.2), calls=%async_computation | async-start | bytes 4096 | tf_op jit(solution)/shard_map/all_to_all | solution.py:74
  21.4 8.7 %all-to-all-start.2 = ((bf16[4,32,2]{1,2,0:T(2,128)(2,1)}), bf16[4,32,2]{1,2,0:T(2,128)(2,1)S(1)}, u32[]{:S(2)}, u32[]{:S(2)}) async-start(bf16[4,32,2]{1,2,0:T(2,128)(2,1)} %convolution_convert_fusion.1), calls=%async_computation.2 | async-start | bytes 4096 | tf_op jit(solution)/shard_map/all_to_all | solution.py:75
  29.3 11.8 %copy-start.5 = (bf16[4,256,128]{2,1,0:T(8,128)(2,1)S(1)}, bf16[4,256,128]{2,1,0:T(8,128)(2,1)}, u32[]{:S(2)}) copy-start(bf16[4,256,128]{2,1,0:T(8,128)(2,1)} %param.9) | copy-start | bytes 786436
  29.3 12.0 %copy-start.6 = (f32[4,31]{1,0:T(4,128)S(1)}, f32[4,31]{1,0:T(4,128)}, u32[]{:S(2)}) copy-start(f32[4,31]{1,0:T(4,128)} %param.10) | copy-start | bytes 1492
  29.3 12.1 %copy-start.7 = (f32[4,31]{1,0:T(4,128)S(1)}, f32[4,31]{1,0:T(4,128)}, u32[]{:S(2)}) copy-start(f32[4,31]{1,0:T(4,128)} %param.11) | copy-start | bytes 1492
  30.1 142.2 %all-to-all-start.1 = ((bf16[4,32,128,128]{3,1,2,0:T(8,128)(2,1)}), bf16[4,32,128,128]{3,1,2,0:T(8,128)(2,1)}, u32[]{:S(2)}, u32[]{:S(2)}) async-start(bf16[4,32,128,128]{3,1,2,0:T(8,128)(2,1)} %copy.88), calls=%async_computation.1 | async-start | bytes 8388608 | tf_op jit(solution)/shard_map/all_to_all | solution.py:73
  34.9 178.1 %all-reduce.4.cloned.1.call-start = ((), (), s32[]{:S(2)}) async-start(), calls=%async_computation.3 | async-start | bytes 131072 | tf_op jit(solution)/shard_map/psum | solution.py:92
  35.0 45.5 %collective-permute-start.1 = (bf16[15,128]{1,0:T(8,128)(2,1)S(1)}, bf16[15,128]{1,0:T(8,128)(2,1)S(1)}, u32[]{:S(2)}, u32[]{:S(2)}) collective-permute-start(bf16[15,128]{1,0:T(8,128)(2,1)S(1)} %get-tuple-element.175), channel_id=1, source_target_pairs={{4,0},{8,4},{12,8},{5,1},{9,5},{13,9},{6,2},{10,6},{14,10},{7,3},{... | collective-permute-start | bytes 11528 | tf_op jit(solution)/shard_map/ppermute | solution.py:17
  36.3 64.5 %collective-permute-start = (bf16[15,128]{1,0:T(8,128)(2,1)S(1)}, bf16[15,128]{1,0:T(8,128)(2,1)S(1)}, u32[]{:S(2)}, u32[]{:S(2)}) collective-permute-start(bf16[15,128]{1,0:T(8,128)(2,1)S(1)} %get-tuple-element.174), channel_id=1, source_target_pairs={{0,4},{4,8},{8,12},{1,5},{5,9},{9,13},{2,6},{6,10},{10,14},{3,7},{... | collective-permute-start | bytes 11528 | tf_op jit(solution)/shard_map/ppermute | solution.py:14
  101.0 4.4 %collective-permute-start.3 = (bf16[286,15]{1,0:T(8,128)(2,1)S(1)}, bf16[286,15]{1,0:T(8,128)(2,1)S(1)}, u32[]{:S(2)}, u32[]{:S(2)}) collective-permute-start(bf16[286,15]{1,0:T(8,128)(2,1)S(1)} %get-tuple-element.171), channel_id=1, source_target_pairs={{2,0},{0,2},{3,1},{1,3},{6,4},{4,6},{7,5},{5,7},{10,8},{8,10},{11,... | collective-permute-start | bytes 25748 | tf_op jit(solution)/shard_map/ppermute | solution.py:17
  102.6 4.4 %collective-permute-start.2 = (bf16[286,15]{1,0:T(8,128)(2,1)S(1)}, bf16[286,15]{1,0:T(8,128)(2,1)S(1)}, u32[]{:S(2)}, u32[]{:S(2)}) collective-permute-start(bf16[286,15]{1,0:T(8,128)(2,1)S(1)} %get-tuple-element.170), channel_id=1, source_target_pairs={{0,2},{2,0},{1,3},{3,1},{4,6},{6,4},{5,7},{7,5},{8,10},{10,8},{9,1... | collective-permute-start | bytes 25748 | tf_op jit(solution)/shard_map/ppermute | solution.py:14
  145.0 10.4 %copy-start.1 = (f32[256,158]{1,0:T(8,128)S(1)}, f32[256,158]{1,0:T(8,128)}, u32[]{:S(2)}) copy-start(f32[256,158]{1,0:T(8,128)} %get-tuple-element.164) | copy-start | bytes 485380
  157.2 10.3 %copy-start.8 = (f32[4]{0:T(128)S(1)}, f32[4]{0:T(128)}, u32[]{:S(2)}) copy-start(f32[4]{0:T(128)} %get-tuple-element.92) | copy-start | bytes 52
  157.2 10.3 %copy-start.9 = (f32[4]{0:T(128)S(1)}, f32[4]{0:T(128)}, u32[]{:S(2)}) copy-start(f32[4]{0:T(128)} %get-tuple-element.93) | copy-start | bytes 52
  157.2 10.3 %copy-start.10 = (f32[4]{0:T(128)S(1)}, f32[4]{0:T(128)}, u32[]{:S(2)}) copy-start(f32[4]{0:T(128)} %get-tuple-element.94) | copy-start | bytes 52
  157.2 10.3 %copy-start.11 = (f32[4]{0:T(128)S(1)}, f32[4]{0:T(128)}, u32[]{:S(2)}) copy-start(f32[4]{0:T(128)} %get-tuple-element.95) | copy-start | bytes 52
  157.2 10.3 %copy-start.12 = (f32[4]{0:T(128)S(1)}, f32[4]{0:T(128)}, u32[]{:S(2)}) copy-start(f32[4]{0:T(128)} %get-tuple-element.96) | copy-start | bytes 52
  172.2 41.7 %copy-start.33 = (f32[256]{0:T(256)S(1)}, f32[256]{0:T(256)}, u32[]{:S(2)}) copy-start(f32[256]{0:T(256)} %broadcast_bitcast_fusion) | copy-start | bytes 3076
  172.2 120.9 %all-reduce.6.cloned.1.call-start = ((), (), s32[]{:S(2)}) async-start(), calls=%async_computation.4 | async-start | bytes 524288 | tf_op jit(solution)/shard_map/psum | solution.py:98
  214.5 16.0 %collective-permute-start.5 = (f32[2,4,15,128]{2,1,3,0:T(4,128)S(1)}, f32[2,4,15,128]{2,1,3,0:T(4,128)S(1)}, u32[]{:S(2)}, u32[]{:S(2)}) collective-permute-start(f32[2,4,15,128]{2,1,3,0:T(4,128)S(1)} %get-tuple-element.134), channel_id=1, source_target_pairs={{4,0},{8,4},{12,8},{5,1},{9,5},{13,9},{6,2},{10,6},{14,10},{7,3},{... | collective-permute-start | bytes 184328 | tf_op jit(solution)/shard_map/ppermute | solution.py:17
  215.8 15.9 %collective-permute-start.4 = (f32[2,4,15,128]{2,1,3,0:T(4,128)S(1)}, f32[2,4,15,128]{2,1,3,0:T(4,128)S(1)}, u32[]{:S(2)}, u32[]{:S(2)}) collective-permute-start(f32[2,4,15,128]{2,1,3,0:T(4,128)S(1)} %get-tuple-element.133), channel_id=1, source_target_pairs={{0,4},{4,8},{8,12},{1,5},{5,9},{9,13},{2,6},{6,10},{10,14},{3,7},{... | collective-permute-start | bytes 184328 | tf_op jit(solution)/shard_map/ppermute | solution.py:14
  232.0 7.6 %collective-permute-start.7 = (f32[2,4,286,15]{2,1,3,0:T(4,128)S(1)}, f32[2,4,286,15]{2,1,3,0:T(4,128)S(1)}, u32[]{:S(2)}, u32[]{:S(2)}) collective-permute-start(f32[2,4,286,15]{2,1,3,0:T(4,128)S(1)} %get-tuple-element.132), channel_id=1, source_target_pairs={{2,0},{0,2},{3,1},{1,3},{6,4},{4,6},{7,5},{5,7},{10,8},{8,10},{11,... | collective-permute-start | bytes 411848 | tf_op jit(solution)/shard_map/ppermute | solution.py:17
  233.8 8.0 %collective-permute-start.6 = (f32[2,4,286,15]{2,1,3,0:T(4,128)S(1)}, f32[2,4,286,15]{2,1,3,0:T(4,128)S(1)}, u32[]{:S(2)}, u32[]{:S(2)}) collective-permute-start(f32[2,4,286,15]{2,1,3,0:T(4,128)S(1)} %get-tuple-element.131), channel_id=1, source_target_pairs={{0,2},{2,0},{1,3},{3,1},{4,6},{6,4},{5,7},{7,5},{8,10},{10,8},{9,1... | collective-permute-start | bytes 411848 | tf_op jit(solution)/shard_map/ppermute | solution.py:14
  (23 other events, 220.1 us)
Sparse Core Ops, SparseCore 0:
  172.3 40.6 all-reduce.3
  272.6 20.4 all-reduce.5
where the time goes:
time: 303 us; the launch traced here: 302 us
  waiting for transfers between devices  138 us (46%)
  local copies, waits for them, and re-layouts  61.5 us (20%)
  other arithmetic  49.7 us (16%)
  starting transfers between devices  30.7 us (10%)
  between operations  14.1 us (5%)
  matrix products  7.66 us (3%)
    ppermute x4, waiting for transfers between devices, extended(): lax.ppermute(lax.slice_in_dim(block, 0, width, axis=dim), axis, backward)  49.9 us
    mul x31, local copies, waits for them, and re-layouts, sweep(): tap_stack[tap_index]  47.9 us
    psum x1, waiting for transfers between devices, body(): lax.psum(partial_value.astype(jnp.bfloat16), 'sub').astype(jnp.float32)  37.7 us
    add x2, other arithmetic, sweep(): running + tap_stack[tap_index] * lax.slice_in_dim(source, tap_index, tap_...  30.9 us
    ppermute x4, waiting for transfers between devices, extended(): lax.ppermute(lax.slice_in_dim(block, block.shape[dim] - width, None, axis...  25.1 us
    psum x1, waiting for transfers between devices, body(): numerator, denominator = lax.psum((backward[0], backward[1]), 'sub')  20.5 us
    ppermute x4, starting transfers between devices, extended(): lax.ppermute(lax.slice_in_dim(block, block.shape[dim] - width, None, axis...  10.4 us
    reduce_sum x1, other arithmetic, body(): jnp.sum(separable(weighted, row_behind, col_behind, tile_rows, block_size...  6.54 us
  transfers between devices with their start and end apart: 13, of which 12 were waited for; matrix products, arithmetic and copies ran while one was open for 27% of the time, Pallas kernels for 0%

commit v1 on v0

--- a/solution.py
+++ b/solution.py
@@ -2,6 +2,7 @@
 import jax.numpy as jnp
 from jax import lax
 from jax.sharding import PartitionSpec as P
+from jax.lax import all_gather
 
 
 def extended(block, sides, width, periodic):
@@ -89,7 +90,8 @@
     partial_value = jnp.sum(
         weight_stack * separable(padded[None], row_ahead, col_ahead, tile_rows, block_size), axis=0
     )
-    smeared_image = lax.psum(partial_value.astype(jnp.bfloat16), "sub").astype(jnp.float32)
+    form_strings = lambda m, net_axis: all_gather(m, axis_name=net_axis).sum(axis=0)
+    smeared_image = form_strings(partial_value.astype(jnp.bfloat16), "sub").astype(jnp.float32)
     quotient = counts / smeared_image
     stacked = jnp.stack([weight_stack * quotient[None], weight_stack * coverage[None]])
     weighted = extended(stacked, (("tube", 2),), margin, False)

time: 303 us -> 288 us (0.950)
  waiting for transfers between devices: 138 us -> 98.9 us
  starting transfers between devices: 30.7 us -> 54.7 us
    psum x1 -> x0, waiting for transfers between devices: 37.7 us -> none  [body(): lax.psum(partial_value.astype(jnp.bfloat16), 'sub').astype(jnp.float32)]
    ppermute x4, starting transfers between devices: 10.4 us -> 35.3 us  [extended(): lax.ppermute(lax.slice_in_dim(block, block.shape[dim] - width, None, axis...]
  transfers between devices with their start and end apart: 13 -> 12, of which waited for: 12 -> 11; matrix products, arithmetic and copies ran while one was open for 27% -> 27% of each run, Pallas kernels for 0% -> 0%
where the time goes in v1:
time: 288 us; the launch traced here: 287 us
  waiting for transfers between devices  98.9 us (34%)
  local copies, waits for them, and re-layouts  61.3 us (21%)
  starting transfers between devices  54.7 us (19%)
  other arithmetic  48.5 us (17%)
  between operations  14.1 us (5%)
  matrix products  7.66 us (3%)
    ppermute x4, waiting for transfers between devices, extended(): lax.ppermute(lax.slice_in_dim(block, 0, width, axis=dim), axis, backward)  50.1 us
    mul x31, local copies, waits for them, and re-layouts, sweep(): tap_stack[tap_index]  47.8 us
    ppermute x4, starting transfers between devices, extended(): lax.ppermute(lax.slice_in_dim(block, block.shape[dim] - width, None, axis...  35.3 us
    add x2, other arithmetic, sweep(): running + tap_stack[tap_index] * lax.slice_in_dim(source, tap_index, tap_...  30.9 us
    ppermute x4, waiting for transfers between devices, extended(): lax.ppermute(lax.slice_in_dim(block, block.shape[dim] - width, None, axis...  25.2 us
    psum x1, waiting for transfers between devices, body(): numerator, denominator = lax.psum((backward[0], backward[1]), 'sub')  18.7 us
    reduce_sum x1, other arithmetic, body(): jnp.sum(separable(weighted, row_behind, col_behind, tile_rows, block_size...  6.54 us
    all_to_all x1, starting transfers between devices, body(): lax.all_to_all(send_places, 'tube', split_axis=0, concat_axis=0, tiled=True)  6.32 us
  transfers between devices with their start and end apart: 12, of which 11 were waited for; matrix products, arithmetic and copies ran while one was open for 27% of the time, Pallas kernels for 0%

profile of v1, /device:TPU:0, one launch (start us, length us, event | category | flops | bytes accessed | tf_op | source)
XLA Modules:
  0.0 287.1 jit_solution(4810684406019213218)
XLA Ops:
  9.6 6.3 %all-to-all-start = ((bf16[4,32,2]{1,2,0:T(2,128)(2,1)}), bf16[4,32,2]{1,2,0:T(2,128)(2,1)S(1)}, u32[]{:S(2)}, u32[]{:S(2)}) async-start(bf16[4,32,2]{1,2,0:T(2,128)(2,1)} %convolution_convert_fusion.2), calls=%async_computation | async-start | bytes 4096 | tf_op jit(solution)/shard_map/all_to_all | solution.py:75
  17.3 4.1 %all-to-all-done = bf16[4,32,2]{1,2,0:T(2,128)(2,1)S(1)} async-done(((bf16[4,32,2]{1,2,0:T(2,128)(2,1)}), bf16[4,32,2]{1,2,0:T(2,128)(2,1)S(1)}, u32[]{:S(2)}, u32[]{:S(2)}) %all-to-all-start) | async-done | bytes 544 | tf_op jit(solution)/shard_map/all_to_all | solution.py:75
  21.4 3.2 %all-to-all-start.2 = ((bf16[4,32,2]{1,2,0:T(2,128)(2,1)}), bf16[4,32,2]{1,2,0:T(2,128)(2,1)S(1)}, u32[]{:S(2)}, u32[]{:S(2)}) async-start(bf16[4,32,2]{1,2,0:T(2,128)(2,1)} %convolution_convert_fusion.1), calls=%async_computation.2 | async-start | bytes 4096 | tf_op jit(solution)/shard_map/all_to_all | solution.py:76
  24.6 1.9 convolution_convert_fusion
  26.5 2.7 copy.127
  30.1 4.8 %all-to-all-start.1 = ((bf16[4,32,128,128]{3,1,2,0:T(8,128)(2,1)}), bf16[4,32,128,128]{3,1,2,0:T(8,128)(2,1)}, u32[]{:S(2)}, u32[]{:S(2)}) async-start(bf16[4,32,128,128]{3,1,2,0:T(8,128)(2,1)} %copy.127), calls=%async_computation.1 | async-start | bytes 8388608 | tf_op jit(solution)/shard_map/all_to_all | solution.py:74
  36.3 4.7 %collective-permute-start = (bf16[15,128]{1,0:T(8,128)(2,1)S(1)}, bf16[15,128]{1,0:T(8,128)(2,1)S(1)}, u32[]{:S(2)}, u32[]{:S(2)}) collective-permute-start(bf16[15,128]{1,0:T(8,128)(2,1)S(1)} %get-tuple-element.174), channel_id=1, source_target_pairs={{0,4},{4,8},{8,12},{1,5},{5,9},{9,13},{2,6},{6,10},{10,14},{3,7},{... | collective-permute-start | bytes 11528 | tf_op jit(solution)/shard_map/ppermute | solution.py:15
  46.5 34.0 %collective-permute-done.1 = bf16[15,128]{1,0:T(8,128)(2,1)S(1)} collective-permute-done((bf16[15,128]{1,0:T(8,128)(2,1)S(1)}, bf16[15,128]{1,0:T(8,128)(2,1)S(1)}, u32[]{:S(2)}, u32[]{:S(2)}) %collective-permute-start.1) | collective-permute-done | bytes 3872 | tf_op jit(solution)/shard_map/ppermute | solution.py:18
  80.6 20.3 %collective-permute-done = bf16[15,128]{1,0:T(8,128)(2,1)S(1)} collective-permute-done((bf16[15,128]{1,0:T(8,128)(2,1)S(1)}, bf16[15,128]{1,0:T(8,128)(2,1)S(1)}, u32[]{:S(2)}, u32[]{:S(2)}) %collective-permute-start) | collective-permute-done | bytes 3872 | tf_op jit(solution)/shard_map/ppermute | solution.py:15
  107.0 2.1 slice_bitcast_fusion.30
  143.2 1.7 copy.140
  144.9 1.8 copy.139
  157.3 10.0 %multiply_add_fusion = f32[4,256,158]{1,0,2:T(4,128)S(1)} fusion(f32[256,158]{0,1:T(8,128)S(1)} %copy-done.2, f32[4]{0:T(128)} %get-tuple-element.99, f32[256,158]{0,1:T(8,128)} %copy.159, f32[4]{0:T(128)} %get-tuple-element.100, f32[256,158]{0,1:T(8,128)} %copy.158, f32[4]{0:T(128)} %get-tuple-element.101, f32[256,158]{0,1:T(8,128)} %copy.157, ...), kind=kLoop, calls=%fused_computation.134 | loop fusion | flops 9869312 | bytes 5663216 | tf_op jit(solution)/shard_map/add | solution.py:26
  167.6 3.8 %fusion.62 = bf16[256,128]{0,1:T(8,128)(2,1)S(1)} fusion(bf16[4,256,128]{1,0,2:T(4,128)(2,1)S(1)} %copy.125, f32[4,256,158]{1,0,2:T(4,128)S(1)} %multiply_add_fusion, f32[4]{0:T(128)S(1)} %copy-done.15, f32[4]{0:T(128)S(1)} %copy-done.16, f32[4]{0:T(128)S(1)} %copy-done.17, f32[4]{0:T(128)S(1)} %copy-done.18, f32[4]{0:T(128)S(1)} %copy-done.19, ...), kind=kLoop, calls=%fused_computation.135 | loop fusion | flops 8355840 | bytes 16581104 | tf_op jit(solution)/shard_map/reduce_sum | solution.py:90
  171.5 1.9 all-gather
  173.8 2.9 %convolution_bitcast_fusion = f32[2,128,128]{2,0,1:T(2,128)S(1)} fusion(bf16[4,32,128,128]{3,1,2,0:T(8,128)(2,1)} %all-to-all-done.1, bf16[4,32,2]{1,2,0:T(2,128)(2,1)S(1)} %all-to-all-done), kind=kOutput, calls=%fused_computation.64 | convolution fusion | flops 8388608 | bytes 4325888 | tf_op jit(solution)/shard_map/tcr,tcxy->rxy/dot_general | solution.py:78
  178.7 28.8 %collective-permute-start.4 = (f32[2,4,15,128]{2,1,3,0:T(4,128)S(1)}, f32[2,4,15,128]{2,1,3,0:T(4,128)S(1)}, u32[]{:S(2)}, u32[]{:S(2)}) collective-permute-start(f32[2,4,15,128]{2,1,3,0:T(4,128)S(1)} %get-tuple-element.133), channel_id=1, source_target_pairs={{0,4},{4,8},{8,12},{1,5},{5,9},{9,13},{2,6},{6,10},{10,14},{3,7},{... | collective-permute-start | bytes 184328 | tf_op jit(solution)/shard_map/ppermute | solution.py:15
  207.9 9.7 %collective-permute-done.5 = f32[2,4,15,128]{2,1,3,0:T(4,128)S(1)} collective-permute-done((f32[2,4,15,128]{2,1,3,0:T(4,128)S(1)}, f32[2,4,15,128]{2,1,3,0:T(4,128)S(1)}, u32[]{:S(2)}, u32[]{:S(2)}) %collective-permute-start.5) | collective-permute-done | bytes 61472 | tf_op jit(solution)/shard_map/ppermute | solution.py:18
  222.0 4.7 %collective-permute-done.7 = f32[2,4,286,15]{2,1,3,0:T(4,128)S(1)} collective-permute-done((f32[2,4,286,15]{2,1,3,0:T(4,128)S(1)}, f32[2,4,286,15]{2,1,3,0:T(4,128)S(1)}, u32[]{:S(2)}, u32[]{:S(2)}) %collective-permute-start.7) | collective-permute-done | bytes 137312 | tf_op jit(solution)/shard_map/ppermute | solution.py:18
  226.7 2.2 collective-permute-done.6
  229.0 2.6 pad_maximum_fusion
  231.5 20.9 %fusion.1 = f32[2,4,256,158]{2,1,3,0:T(4,128)S(1)} fusion(f32[2,4,286,158]{2,1,3,0:T(4,128)S(1)} %pad_maximum_fusion, f32[4]{0:T(128)S(1)} %get-tuple-element.37, f32[4]{0:T(128)S(1)} %get-tuple-element.38, f32[4]{0:T(128)S(1)} %get-tuple-element.39, f32[4]{0:T(128)S(1)} %get-tuple-element.40, f32[4]{0:T(128)S(1)} %get-tuple-element.41, ...), kind=kLoop, calls=%fused_computation.4 | loop fusion | flops 19738624 | bytes 41419248 | tf_op jit(solution)/shard_map/add | solution.py:26
  252.4 6.5 %fusion.32 = f32[2,256,128]{1,2,0:T(8,128)S(1)} fusion(f32[2,4,256,158]{2,1,3,0:T(4,128)S(1)} %fusion.1, f32[4]{0:T(128)S(1)} %get-tuple-element.6, f32[4]{0:T(128)S(1)} %get-tuple-element.7, f32[4]{0:T(128)S(1)} %get-tuple-element.8, f32[4]{0:T(128)S(1)} %get-tuple-element.9, f32[4]{0:T(128)S(1)} %get-tuple-element.10, f32[4]{0:T(128)S(1)} %get-tuple-element.11, ...), kind=kLoop, calls=%fused_computation.69 | loop fusion | flops 16187392 | bytes 32768496 | tf_op jit(solution)/shard_map/reduce_sum | solution.py:99
  259.8 18.7 %all-reduce.3.cloned.1.call-done = (f32[256,128]{0,1:T(8,128)}, f32[256,128]{0,1:T(8,128)}) async-done(((f32[256,128]{0,1:T(8,128)}, f32[256,128]{0,1:T(8,128)}), (f32[256,128]{0,1:T(8,128)}, f32[256,128]{0,1:T(8,128)})) %all-reduce.3.cloned.1.call-update) | async-done | bytes 262160 | tf_op jit(solution)/shard_map/psum | solution.py:100
  (152 shorter events, 72.5 us)
Async XLA Ops:
  6.5 18.1 %copy-start = (bf16[1,64,128,128]{3,2,1,0:T(8,128)(2,1)S(1)}, bf16[1,64,128,128]{3,2,1,0:T(8,128)(2,1)}, u32[]{:S(2)}) copy-start(bf16[1,64,128,128]{3,2,1,0:T(8,128)(2,1)} %param.12) | copy-start | bytes 6291460
  9.6 11.8 %all-to-all-start = ((bf16[4,32,2]{1,2,0:T(2,128)(2,1)}), bf16[4,32,2]{1,2,0:T(2,128)(2,1)S(1)}, u32[]{:S(2)}, u32[]{:S(2)}) async-start(bf16[4,32,2]{1,2,0:T(2,128)(2,1)} %convolution_convert_fusion.2), calls=%async_computation | async-start | bytes 4096 | tf_op jit(solution)/shard_map/all_to_all | solution.py:75
  21.4 8.7 %all-to-all-start.2 = ((bf16[4,32,2]{1,2,0:T(2,128)(2,1)}), bf16[4,32,2]{1,2,0:T(2,128)(2,1)S(1)}, u32[]{:S(2)}, u32[]{:S(2)}) async-start(bf16[4,32,2]{1,2,0:T(2,128)(2,1)} %convolution_convert_fusion.1), calls=%async_computation.2 | async-start | bytes 4096 | tf_op jit(solution)/shard_map/all_to_all | solution.py:76
  29.3 11.8 %copy-start.5 = (bf16[4,256,128]{2,1,0:T(8,128)(2,1)S(1)}, bf16[4,256,128]{2,1,0:T(8,128)(2,1)}, u32[]{:S(2)}) copy-start(bf16[4,256,128]{2,1,0:T(8,128)(2,1)} %param.9) | copy-start | bytes 786436
  29.3 12.0 %copy-start.6 = (f32[4,31]{1,0:T(4,128)S(1)}, f32[4,31]{1,0:T(4,128)}, u32[]{:S(2)}) copy-start(f32[4,31]{1,0:T(4,128)} %param.10) | copy-start | bytes 1492
  29.3 12.1 %copy-start.7 = (f32[4,31]{1,0:T(4,128)S(1)}, f32[4,31]{1,0:T(4,128)}, u32[]{:S(2)}) copy-start(f32[4,31]{1,0:T(4,128)} %param.11) | copy-start | bytes 1492
  30.1 143.7 %all-to-all-start.1 = ((bf16[4,32,128,128]{3,1,2,0:T(8,128)(2,1)}), bf16[4,32,128,128]{3,1,2,0:T(8,128)(2,1)}, u32[]{:S(2)}, u32[]{:S(2)}) async-start(bf16[4,32,128,128]{3,1,2,0:T(8,128)(2,1)} %copy.127), calls=%async_computation.1 | async-start | bytes 8388608 | tf_op jit(solution)/shard_map/all_to_all | solution.py:74
  34.9 243.5 %all-reduce.3.cloned.1.call-start = ((), (), s32[]{:S(2)}) async-start(), calls=%async_computation.3 | async-start | bytes 524288 | tf_op jit(solution)/shard_map/psum | solution.py:100
  35.0 45.5 %collective-permute-start.1 = (bf16[15,128]{1,0:T(8,128)(2,1)S(1)}, bf16[15,128]{1,0:T(8,128)(2,1)S(1)}, u32[]{:S(2)}, u32[]{:S(2)}) collective-permute-start(bf16[15,128]{1,0:T(8,128)(2,1)S(1)} %get-tuple-element.175), channel_id=1, source_target_pairs={{4,0},{8,4},{12,8},{5,1},{9,5},{13,9},{6,2},{10,6},{14,10},{7,3},{... | collective-permute-start | bytes 11528 | tf_op jit(solution)/shard_map/ppermute | solution.py:18
  36.3 64.5 %collective-permute-start = (bf16[15,128]{1,0:T(8,128)(2,1)S(1)}, bf16[15,128]{1,0:T(8,128)(2,1)S(1)}, u32[]{:S(2)}, u32[]{:S(2)}) collective-permute-start(bf16[15,128]{1,0:T(8,128)(2,1)S(1)} %get-tuple-element.174), channel_id=1, source_target_pairs={{0,4},{4,8},{8,12},{1,5},{5,9},{9,13},{2,6},{6,10},{10,14},{3,7},{... | collective-permute-start | bytes 11528 | tf_op jit(solution)/shard_map/ppermute | solution.py:15
  101.0 4.4 %collective-permute-start.3 = (bf16[286,15]{1,0:T(8,128)(2,1)S(1)}, bf16[286,15]{1,0:T(8,128)(2,1)S(1)}, u32[]{:S(2)}, u32[]{:S(2)}) collective-permute-start(bf16[286,15]{1,0:T(8,128)(2,1)S(1)} %get-tuple-element.171), channel_id=1, source_target_pairs={{2,0},{0,2},{3,1},{1,3},{6,4},{4,6},{7,5},{5,7},{10,8},{8,10},{11,... | collective-permute-start | bytes 25748 | tf_op jit(solution)/shard_map/ppermute | solution.py:18
  102.6 4.4 %collective-permute-start.2 = (bf16[286,15]{1,0:T(8,128)(2,1)S(1)}, bf16[286,15]{1,0:T(8,128)(2,1)S(1)}, u32[]{:S(2)}, u32[]{:S(2)}) collective-permute-start(bf16[286,15]{1,0:T(8,128)(2,1)S(1)} %get-tuple-element.170), channel_id=1, source_target_pairs={{0,2},{2,0},{1,3},{3,1},{4,6},{6,4},{5,7},{7,5},{8,10},{10,8},{9,1... | collective-permute-start | bytes 25748 | tf_op jit(solution)/shard_map/ppermute | solution.py:15
  144.9 10.4 %copy-start.1 = (f32[256,158]{1,0:T(8,128)S(1)}, f32[256,158]{1,0:T(8,128)}, u32[]{:S(2)}) copy-start(f32[256,158]{1,0:T(8,128)} %get-tuple-element.164) | copy-start | bytes 485380
  157.1 10.3 %copy-start.8 = (f32[4]{0:T(128)S(1)}, f32[4]{0:T(128)}, u32[]{:S(2)}) copy-start(f32[4]{0:T(128)} %get-tuple-element.92) | copy-start | bytes 52
  157.1 10.3 %copy-start.9 = (f32[4]{0:T(128)S(1)}, f32[4]{0:T(128)}, u32[]{:S(2)}) copy-start(f32[4]{0:T(128)} %get-tuple-element.93) | copy-start | bytes 52
  157.1 10.3 %copy-start.10 = (f32[4]{0:T(128)S(1)}, f32[4]{0:T(128)}, u32[]{:S(2)}) copy-start(f32[4]{0:T(128)} %get-tuple-element.94) | copy-start | bytes 52
  157.1 10.3 %copy-start.11 = (f32[4]{0:T(128)S(1)}, f32[4]{0:T(128)}, u32[]{:S(2)}) copy-start(f32[4]{0:T(128)} %get-tuple-element.95) | copy-start | bytes 52
  157.1 10.3 %copy-start.12 = (f32[4]{0:T(128)S(1)}, f32[4]{0:T(128)}, u32[]{:S(2)}) copy-start(f32[4]{0:T(128)} %get-tuple-element.96) | copy-start | bytes 52
  157.1 10.3 %copy-start.13 = (f32[4]{0:T(128)S(1)}, f32[4]{0:T(128)}, u32[]{:S(2)}) copy-start(f32[4]{0:T(128)} %get-tuple-element.97) | copy-start | bytes 52
  157.2 10.3 %copy-start.14 = (f32[4]{0:T(128)S(1)}, f32[4]{0:T(128)}, u32[]{:S(2)}) copy-start(f32[4]{0:T(128)} %get-tuple-element.67) | copy-start | bytes 52
  177.4 40.2 %collective-permute-start.5 = (f32[2,4,15,128]{2,1,3,0:T(4,128)S(1)}, f32[2,4,15,128]{2,1,3,0:T(4,128)S(1)}, u32[]{:S(2)}, u32[]{:S(2)}) collective-permute-start(f32[2,4,15,128]{2,1,3,0:T(4,128)S(1)} %get-tuple-element.134), channel_id=1, source_target_pairs={{4,0},{8,4},{12,8},{5,1},{9,5},{13,9},{6,2},{10,6},{14,10},{7,3},{... | collective-permute-start | bytes 184328 | tf_op jit(solution)/shard_map/ppermute | solution.py:18
  178.7 40.0 %collective-permute-start.4 = (f32[2,4,15,128]{2,1,3,0:T(4,128)S(1)}, f32[2,4,15,128]{2,1,3,0:T(4,128)S(1)}, u32[]{:S(2)}, u32[]{:S(2)}) collective-permute-start(f32[2,4,15,128]{2,1,3,0:T(4,128)S(1)} %get-tuple-element.133), channel_id=1, source_target_pairs={{0,4},{4,8},{8,12},{1,5},{5,9},{9,13},{2,6},{6,10},{10,14},{3,7},{... | collective-permute-start | bytes 184328 | tf_op jit(solution)/shard_map/ppermute | solution.py:15
  219.1 7.6 %collective-permute-start.7 = (f32[2,4,286,15]{2,1,3,0:T(4,128)S(1)}, f32[2,4,286,15]{2,1,3,0:T(4,128)S(1)}, u32[]{:S(2)}, u32[]{:S(2)}) collective-permute-start(f32[2,4,286,15]{2,1,3,0:T(4,128)S(1)} %get-tuple-element.132), channel_id=1, source_target_pairs={{2,0},{0,2},{3,1},{1,3},{6,4},{4,6},{7,5},{5,7},{10,8},{8,10},{11,... | collective-permute-start | bytes 411848 | tf_op jit(solution)/shard_map/ppermute | solution.py:18
  219.9 9.0 %collective-permute-start.6 = (f32[2,4,286,15]{2,1,3,0:T(4,128)S(1)}, f32[2,4,286,15]{2,1,3,0:T(4,128)S(1)}, u32[]{:S(2)}, u32[]{:S(2)}) collective-permute-start(f32[2,4,286,15]{2,1,3,0:T(4,128)S(1)} %get-tuple-element.131), channel_id=1, source_target_pairs={{0,2},{2,0},{1,3},{3,1},{4,6},{6,4},{5,7},{7,5},{8,10},{10,8},{9,1... | collective-permute-start | bytes 411848 | tf_op jit(solution)/shard_map/ppermute | solution.py:15
  (22 other events, 202.5 us)
Sparse Core Ops, SparseCore 0:
  259.8 18.6 all-reduce.2
